TPU v7x, 32 devices: a whole 2x2x4 slice. The times are simulated.
32 devices in a mesh: groups: 2 (over y), row: 4 (over z), col: 4 (over x, core).
Axes of the slice: x: 2, y: 2, z: 4, core: 2. Of those that a mesh axis runs over, the one named last changes fastest.
Arguments:
- hidden: bfloat16 [2048, 8192], P(('groups', 'col'), 'row'), parts along dimension 0, may hold values from -6 to 6
- grad_out: bfloat16 [2048, 4096], P(('groups', 'row'), 'col'), parts along dimension 0, may hold values from -6 to 6
- example_ids: int32 [2048], P(('groups', 'col')), parts along dimension 0, may hold values from 0 to 1, never falling along the last dimension, each value on 1 to 768 neighbouring positions
- sign_bits: int32 [8192, 4096], P('row', 'col'), may hold values from 0 to 1
- sample_index: int32 [8192], replicated, may hold values from 0 to 33554431
Outputs:
- projections: float32 [4, 8192], P('groups', ('row', 'col')), parts along dimension 0
There are 2 independent parts, one for each index of `groups`. A program takes and returns all parts, laid end to end along the dimension named above; an argument that names none is the same for every part. Nothing has to cross between parts.
Inputs may be any that keep to these rules, and one draw needn't show every extreme that they name: `example_ids`: example ids never fall along the tokens; every example has at least one token.
All inputs are finite; a program needn't handle non-finite values.
Results may differ from a plain program's by a relative error of at most 0.0003.
Values may be sent and summed in bfloat16 or wider, within the bound.
A program may use at most 320 MiB of HBM per device.

v0:
```python
import math

import jax
import jax.numpy as jnp
from jax import lax
from jax.sharding import PartitionSpec as P

EXAMPLES = 2
TOK_EX = 512


def sylvester(order):
    position = jnp.arange(order, dtype=jnp.int32)
    parity = jnp.zeros((order, order), jnp.int32)
    for level in range(order.bit_length() - 1):
        parity = parity + (position[:, None] >> level & 1) * (position[None, :] >> level & 1)
    return (1 - 2 * (parity % 2)).astype(jnp.float32)


def shards(hidden, grad_out, example_ids, sign_bits, sample_index):
    row_block = hidden.shape[1]
    col_block = grad_out.shape[1]
    row_count = lax.axis_size("row")
    col_count = lax.axis_size("col")
    d_total = col_block * col_count
    grad_all = lax.all_gather(grad_out, "row", axis=0, tiled=True)
    labels = jnp.arange(EXAMPLES, dtype=jnp.int32)
    piece_hidden = lax.all_gather(hidden, "col", axis=0, tiled=True)
    piece_ids = lax.all_gather(example_ids, "col", axis=0, tiled=True)
    count = piece_hidden.shape[0]
    onehot = (piece_ids[:, None] == labels[None, :]).astype(jnp.bfloat16)
    masked = (onehot[:, :, None] * piece_hidden[:, None, :]).reshape(count, EXAMPLES * row_block)
    grads = lax.dot_general(
        masked, grad_all, (((0,), (0,)), ((), ())), preferred_element_type=jnp.float32
    )
    scale = 1.0 / math.sqrt(row_block * row_count * d_total * TOK_EX)
    signs = (1 - 2 * sign_bits).astype(jnp.float32)
    flipped = grads.reshape(EXAMPLES, row_block, col_block) * signs[None] * scale
    highest = lax.Precision.HIGHEST
    local = jnp.einsum("ij,ejk->eik", sylvester(row_block), flipped, precision=highest)
    local = jnp.einsum("eik,kl->eil", local, sylvester(col_block), precision=highest)
    row_pos = lax.axis_index("row")
    col_pos = lax.axis_index("col")
    row_global = sample_index // d_total
    col_global = sample_index % d_total
    row_owner = row_global // row_block
    row_inner = row_global % row_block
    col_owner = col_global // col_block
    col_inner = col_global % col_block
    flat_inner = row_inner * col_block + col_inner
    row_table = sylvester(row_count)
    col_table = sylvester(col_count)
    stacked = local.reshape(EXAMPLES, 1, row_block, col_block)
    mixed = jnp.einsum(
        "ij,ejrc->eirc",
        row_table,
        lax.all_to_all(stacked, "row", split_axis=3, concat_axis=1, tiled=True),
        precision=highest,
    )
    stacked = lax.all_to_all(mixed, "row", split_axis=1, concat_axis=3, tiled=True)
    mixed = jnp.einsum(
        "ij,ejrc->eirc",
        col_table,
        lax.all_to_all(stacked, "col", split_axis=2, concat_axis=1, tiled=True),
        precision=highest,
    )
    stacked = lax.all_to_all(mixed, "col", split_axis=1, concat_axis=2, tiled=True)
    whole = stacked.reshape(EXAMPLES, row_block * col_block)
    owner = (row_owner == row_pos) & (col_owner == col_pos)
    terms = jnp.where(owner[None, :], jnp.take(whole, flat_inner, axis=1), 0.0)
    return lax.psum_scatter(terms, ("row", "col"), scatter_dimension=1, tiled=True)


def solution(mesh):
    placed = (
        P(("groups", "col"), "row"),
        P(("groups", "row"), "col"),
        P(("groups", "col")),
        P("row", "col"),
        P(),
    )
    return jax.shard_map(
        shards, mesh=mesh, in_specs=placed, out_specs=P("groups", ("row", "col")), check_vma=False
    )
```

profile of v0, /device:TPU:0, one launch (start us, length us, event | category | flops | bytes accessed | tf_op | source)
XLA Modules:
  0.0 1954.7 jit_solution(3151187747665954397)
XLA Ops:
  6.5 0.7 all-gather.4.cloned.1.call-update
  7.3 0.7 all-gather.6.cloned.1.call-update
  8.0 6.3 all-gather
  14.4 8.8 subtract_convert_fusion
  23.2 6.4 fusion.148
  29.6 16.6 all-gather.4.cloned.1.call-done
  46.1 6.4 copy.18
  52.5 41.1 %all-gather.6.cloned.1.call-done = bf16[1024,1024]{1,0:T(8,128)(2,1)} async-done(((bf16[256,1024]{1,0:T(8,128)(2,1)}), bf16[1024,1024]{1,0:T(8,128)(2,1)}) %all-gather.6.cloned.1.call-update) | async-done | bytes 2097168 | tf_op jit(solution)/shard_map/all_gather | solution.py:26
  93.7 14.9 fusion.24
  108.5 14.7 fusion.146
  123.2 256.5 %fusion.5 = f32[2,1024,2048]{2,1,0:T(8,128)} fusion(s32[2048]{0:T(1024)S(1)} %get-tuple-element.8, s32[2048]{0:T(1024)S(1)} %get-tuple-element.9, s32[2048]{0:T(1024)S(1)} %get-tuple-element.10, s32[2048]{0:T(1024)S(1)} %get-tuple-element.11, s32[2048]{0:T(1024)S(1)} %get-tuple-element.12, s32[2048]{0:T(1024)S(1)} %get-tuple-element.13, ...), kind=kOutput, calls=%fused_computation.9 | convolution fusion | flops 103226015744 | bytes 33644544 | tf_op jit(solution)/shard_map/ij,ejk->eik/dot_general | solution.py:40
  379.8 59.4 %fusion.54 = f32[2,1,2048,1024]{3,2,0,1:T(8,128)} fusion(f32[2,1024,2048]{2,1,0:T(8,128)} %fusion.5, f32[1024,1024,1]{1,0,2:T(8,128)S(1)} %copy-done), kind=kOutput, calls=%fused_computation.54 | convolution fusion | flops 51539607552 | bytes 37748736 | tf_op jit(solution)/shard_map/eik,kl->eil/dot_general | solution.py:41
  439.2 25.4 %copy.21 = f32[2,1,2048,1024]{2,0,1,3:T(2,128)} copy(f32[2,1,2048,1024]{3,2,0,1:T(8,128)} %fusion.54) | data formatting | bytes 33554432 | tf_op jit(solution)/shard_map/reshape | solution.py:53
  464.6 7.0 all-to-all-start
  471.6 363.1 %all-to-all-done = f32[2,1,2048,1024]{2,0,1,3:T(2,128)} async-done(((f32[2,1,2048,1024]{2,0,1,3:T(2,128)}), f32[2,1,2048,1024]{2,0,1,3:T(2,128)}, u32[]{:S(2)}, u32[]{:S(2)}) %all-to-all-start) | async-done | bytes 16777248 | tf_op jit(solution)/shard_map/all_to_all | solution.py:57
  834.7 25.8 %copy.33 = f32[2,1,2048,4,256]{4,3,2,0,1:T(4,128)} copy(f32[2,1,2048,4,256]{2,0,4,3,1:T(2,128)} %bitcast.10) | data formatting | bytes 33554432 | tf_op jit(solution)/shard_map/all_to_all | solution.py:57
  860.5 32.7 %fusion.18 = f32[2,4,2048,256]{3,1,2,0:T(4,128)S(1)} fusion(f32[2,1,2048,4,256]{4,3,2,0,1:T(4,128)} %copy.33, s32[4]{0:T(128)S(1)} %get-tuple-element.28, s32[4]{0:T(128)S(1)} %get-tuple-element.29), kind=kOutput, calls=%fused_computation.21 | convolution fusion | flops 201326864 | bytes 33554464 | tf_op jit(solution)/shard_map/ij,ejrc->eirc/dot_general | solution.py:54
  893.2 8.1 copy.23
  901.3 366.7 %all_to_all.57 = f32[2,4,2048,256]{3,2,0,1:T(8,128)} all-to-all(f32[2,4,2048,256]{3,2,0,1:T(8,128)S(1)} %copy.23), channel_id=1, replica_groups=mesh['groups'=2,'row'=4,'col'=4] {'row'}, dimensions={1} | all-to-all | bytes 33554432 | tf_op jit(solution)/shard_map/all_to_all | solution.py:60
  1268.0 16.6 copy.24
  1284.6 25.4 %copy.25 = f32[2,1,2048,1024]{3,0,1,2:T(2,128)} copy(f32[2,1,2048,1024]{2,3,0,1:T(8,128)} %bitcast.67) | data formatting | bytes 33554432 | tf_op jit(solution)/shard_map/all_to_all | solution.py:60
  1310.0 188.1 %all_to_all.58 = f32[2,1,2048,1024]{3,0,1,2:T(2,128)S(1)} all-to-all(f32[2,1,2048,1024]{3,0,1,2:T(2,128)} %copy.25), channel_id=1, replica_groups=mesh['groups'=2,'row'=4,'col'=4] {'col'}, dimensions={2} | all-to-all | bytes 33554432 | tf_op jit(solution)/shard_map/all_to_all | solution.py:64
  1498.2 43.7 %fusion.21 = f32[2,4,512,1024]{3,1,2,0:T(4,128)} fusion(f32[2,4,512,1024]{3,0,2,1:T(2,128)S(1)} %bitcast.66, s32[4]{0:T(128)S(1)} %get-tuple-element.28, s32[4]{0:T(128)S(1)} %get-tuple-element.29), kind=kOutput, calls=%fused_computation.22 | convolution fusion | flops 201326864 | bytes 33554464 | tf_op jit(solution)/shard_map/ij,ejrc->eirc/dot_general | solution.py:61
  1541.8 17.7 copy.28
  1559.6 7.1 all-to-all-start.3
  1566.9 182.9 %all-to-all-done.3 = f32[2,4,512,1024]{3,2,0,1:T(8,128)} async-done(((f32[2,4,512,1024]{3,2,0,1:T(8,128)}), f32[2,4,512,1024]{3,2,0,1:T(8,128)}, u32[]{:S(2)}, u32[]{:S(2)}) %all-to-all-start.3) | async-done | bytes 16777248 | tf_op jit(solution)/shard_map/all_to_all | solution.py:67
  1749.7 6.7 copy.29
  1756.5 25.1 %copy.38 = f32[1,2,2048,1024]{3,1,2,0:T(2,128)} copy(f32[1,2,2048,1024]{3,2,1,0:T(8,128)S(1)} %bitcast.68) | data formatting | bytes 33554432
  1781.6 91.4 %gather_fusion = f32[8192,2]{0,1:T(2,128)S(1)} fusion(f32[2,2097152]{1,0:T(2,128)} %bitcast.69, s32[8192]{0:T(1024)S(1)} %broadcast_clamp_fusion), kind=kCustom, calls=%fused_computation | custom fusion | bytes 163840 | tf_op jit(solution)/shard_map/jit(_take)/gather | solution.py:70
  1873.0 2.6 copy.36
  1875.7 70.7 %reduce-scatter.4.cloned.1.call-done = f32[512,2]{1,0:T(8,128)} async-done(((f32[8192,2]{1,0:T(8,128)}), f32[512,2]{1,0:T(8,128)}) %reduce-scatter.4.cloned.1.call-update) | async-done | bytes 4112
  1946.4 1.7 copy.37
  (24 shorter events, 0.4 us)
Async XLA Ops:
  6.5 39.6 %all-gather.4.cloned.1.call-start = ((), (), s32[]{:S(2)}) async-start(), calls=%async_computation.5 | async-start | bytes 5242880 | tf_op jit(solution)/shard_map/all_gather | solution.py:28
  7.3 86.4 %all-gather.6.cloned.1.call-start = ((), (), s32[]{:S(2)}) async-start(), calls=%async_computation.6 | async-start | bytes 2621440 | tf_op jit(solution)/shard_map/all_gather | solution.py:26
  123.2 256.5 %copy-start = (f32[1024,1024,1]{1,0,2:T(8,128)S(1)}, f32[1024,1024,1]{1,0,2:T(8,128)}, u32[]{:S(2)}) copy-start(f32[1024,1024,1]{1,0,2:T(8,128)} %fusion.148) | copy-start | bytes 12582916
  464.6 370.1 %all-to-all-start = ((f32[2,1,2048,1024]{2,0,1,3:T(2,128)}), f32[2,1,2048,1024]{2,0,1,3:T(2,128)}, u32[]{:S(2)}, u32[]{:S(2)}) async-start(f32[2,1,2048,1024]{2,0,1,3:T(2,128)} %copy.21), calls=%async_computation | async-start | bytes 33554432 | tf_op jit(solution)/shard_map/all_to_all | solution.py:57
  1559.6 7.2 copy-start.1
  1559.6 190.2 %all-to-all-start.3 = ((f32[2,4,512,1024]{3,2,0,1:T(8,128)}), f32[2,4,512,1024]{3,2,0,1:T(8,128)}, u32[]{:S(2)}, u32[]{:S(2)}) async-start(f32[2,4,512,1024]{3,2,0,1:T(8,128)} %copy.28), calls=%async_computation.3 | async-start | bytes 33554432 | tf_op jit(solution)/shard_map/all_to_all | solution.py:67
  1566.7 379.7 %reduce-scatter.4.cloned.1.call-start = ((), (), s32[]{:S(2)}) async-start(), calls=%async_computation.7 | async-start | bytes 4456448
Sparse Core Ops, SparseCore 0:
  8.9 37.1 all-gather.3
  47.7 45.9 all-gather.5
  1875.8 70.5 reduce-scatter.3
where the time goes:
time: 1970 us; the launch traced here: 1950 us
  waiting for transfers between devices  676 us (34%)
  blocking collectives  561 us (28%)
  matrix products  407 us (21%)
  local copies, waits for them, and re-layouts  253 us (13%)
  other arithmetic  30.1 us (2%)
    all_to_all x1, blocking collectives, shards(): lax.all_to_all(mixed, 'row', split_axis=1, concat_axis=3, tiled=True)  367 us
    all_to_all x1, waiting for transfers between devices, shards(): lax.all_to_all(stacked, 'row', split_axis=3, concat_axis=1, tiled=True)  363 us
    dot_general x1, matrix products, shards(): jnp.einsum('ij,ejk->eik', sylvester(row_block), flipped, precision=highest)  257 us
    all_to_all x1, blocking collectives, shards(): lax.all_to_all(stacked, 'col', split_axis=2, concat_axis=1, tiled=True)  188 us
    all_to_all x1, waiting for transfers between devices, shards(): lax.all_to_all(mixed, 'col', split_axis=1, concat_axis=2, tiled=True)  183 us
    gather x1, local copies, waits for them, and re-layouts, shards(): terms = jnp.where(owner[None, :], jnp.take(whole, flat_inner, axis=1), 0.0)  91.4 us
    unnamed x4, waiting for transfers between devices  72.1 us
    dot_general x1, matrix products, shards(): jnp.einsum('eik,kl->eil', local, sylvester(col_block), precision=highest)  59.4 us
  transfers between devices with their start and end apart: 5, of which 5 were waited for; matrix products, arithmetic and copies ran while one was open for 1% of the time, Pallas kernels for 0%

commit v1 on v0

v1 whole, which is shorter than its diff:
```python
import functools
import math

import jax
import jax.numpy as jnp
import numpy as np
from jax import lax
from jax.experimental import pallas as pl
from jax.experimental.pallas import tpu as pltpu
from jax.sharding import PartitionSpec as P

EXAMPLES = 2
TOK_EX = 512
LANES = 128
WIDE = 256
UNROLL = 16
BATCH = 1024


def sylvester(order):
    table = np.ones((1, 1), np.float32)
    while table.shape[0] < order:
        table = np.block([[table, table], [table, -table]])
    return jnp.asarray(table, jnp.bfloat16)


def butterfly(values):
    span = 1
    values = list(values)
    while span < len(values):
        for start in range(0, len(values), 2 * span):
            for i in range(start, start + span):
                a, b = values[i], values[i + span]
                values[i], values[i + span] = a + b, a - b
        span *= 2
    return values


def split(values):
    high = values.astype(jnp.bfloat16)
    return high, (values - high.astype(jnp.float32)).astype(jnp.bfloat16)


def kernel(
    order, place_ref, ids_ref, low_ref, hidden_ref, grad_ref, sign_ref, pair_ref, lane_ref,
    out_ref, table, flipped, parts, picked,
):
    step = pl.program_id(0)
    rows = hidden_ref.shape[0]
    blocks = rows // order
    chunks = table.shape[1]
    samples = low_ref.shape[1]

    labels = ids_ref[...]
    for e in range(EXAMPLES):
        masked = jnp.where(labels == e, grad_ref[...].astype(jnp.float32), 0.0).astype(jnp.bfloat16)

        def multiply(b, _):
            at = pl.ds(pl.multiple_of(b * order, order), order)
            grads = jnp.dot(hidden_ref[at, :], masked, preferred_element_type=jnp.float32)
            flipped[b] = jnp.where(sign_ref[at, :] == 0, grads, -grads)
            return 0

        lax.fori_loop(0, blocks, multiply, 0)

        def mix(i, _):
            at = pl.ds(pl.multiple_of(i * 16, 16), 16)
            below = pl.ds(pl.multiple_of(order + i * 16, 16), 16)
            values = butterfly([flipped[b, at, :] for b in range(blocks)])
            for b in range(blocks):
                high, low = split(values[b])
                parts[b, at, :] = high
                parts[b, below, :] = low
            return 0

        lax.fori_loop(0, order // 16, mix, 0)

        def transform(b, _):
            at = pl.ds(pl.multiple_of(b * order, order), order)
            values = jnp.dot(pair_ref[...], parts[b], preferred_element_type=jnp.float32)
            for half in range(WIDE // LANES):
                table[e, step * (WIDE // LANES) + half, at, :] = values[:, half * LANES:(half + 1) * LANES]
            return 0

        lax.fori_loop(0, blocks, transform, 0)

    @pl.when(step == pl.num_programs(0) - 1)
    def _():
        for e in range(EXAMPLES):
            def across(i, _):
                at = pl.ds(pl.multiple_of(i * 16, 16), 16)
                values = butterfly([table[e, c, at, :] for c in range(chunks)])
                for c in range(chunks):
                    table[e, c, at, :] = values[c]
                return 0

            lax.fori_loop(0, rows // 16, across, 0)

        flat = table.reshape(EXAMPLES, chunks * rows, LANES)
        lane = lax.broadcasted_iota(jnp.int32, (LANES, BATCH), 0)

        def sample(n, _):
            base = n * BATCH

            def pick(i, _):
                for u in range(UNROLL):
                    k = i * UNROLL + u
                    place = place_ref[base + k]
                    for e in range(EXAMPLES):
                        picked[e, pl.ds(k, 1), :] = flat[e, pl.ds(place, 1), :]
                return 0

            lax.fori_loop(0, BATCH // UNROLL, pick, 0)
            at = pl.ds(pl.multiple_of(base, BATCH), BATCH)
            keep = lane == low_ref[:, at]
            for e in range(EXAMPLES):
                high, low = split(picked[e])
                dims = (((1,), (1,)), ((), ()))
                values = lax.dot_general(lane_ref[...], high, dims, preferred_element_type=jnp.float32)
                values = values + lax.dot_general(lane_ref[...], low, dims, preferred_element_type=jnp.float32)
                out_ref[e:e + 1, at] = jnp.sum(jnp.where(keep, values, 0.0), axis=0, keepdims=True)
            return 0

        lax.fori_loop(0, samples // BATCH, sample, 0)


def sketch(hidden, grad, ids, sign_bits, place, low):
    rows, tokens = hidden.shape
    columns = grad.shape[1]
    order = min(rows, 256)
    chunks = columns // LANES
    whole = lambda j, place: (0, 0)
    half = sylvester(order)
    return pl.pallas_call(
        functools.partial(kernel, order),
        out_shape=jax.ShapeDtypeStruct((EXAMPLES, low.shape[1]), jnp.float32),
        grid_spec=pltpu.PrefetchScalarGridSpec(
            num_scalar_prefetch=1,
            grid=(columns // WIDE,),
            in_specs=[
                pl.BlockSpec((tokens, 1), whole),
                pl.BlockSpec((1, low.shape[1]), whole),
                pl.BlockSpec((rows, tokens), whole),
                pl.BlockSpec((tokens, WIDE), lambda j, place: (0, j)),
                pl.BlockSpec((rows, WIDE), lambda j, place: (0, j)),
                pl.BlockSpec((order, 2 * order), whole),
                pl.BlockSpec((LANES, LANES), whole),
            ],
            out_specs=pl.BlockSpec((EXAMPLES, low.shape[1]), whole),
            scratch_shapes=[
                pltpu.VMEM((EXAMPLES, chunks, rows, LANES), jnp.float32),
                pltpu.VMEM((rows // order, order, WIDE), jnp.float32),
                pltpu.VMEM((rows // order, 2 * order, WIDE), jnp.bfloat16),
                pltpu.VMEM((EXAMPLES, BATCH, LANES), jnp.float32),
            ],
        ),
        compiler_params=pltpu.CompilerParams(vmem_limit_bytes=56 << 20),
        name="sketch",
    )(place, ids, low, hidden, grad, sign_bits, jnp.concatenate([half, half], axis=1), sylvester(LANES))


def shards(hidden, grad_out, example_ids, sign_bits, sample_index):
    row_block = hidden.shape[1]
    col_block = grad_out.shape[1]
    row_count = lax.axis_size("row")
    col_count = lax.axis_size("col")
    d_total = col_block * col_count
    grad_all = lax.all_gather(grad_out, "row", axis=0, tiled=True)
    hidden_all = lax.all_gather(hidden.T, "col", axis=1, tiled=True)
    ids = lax.all_gather(example_ids, "col", axis=0, tiled=True)
    row_global = sample_index // d_total
    col_global = sample_index % d_total
    row_inner = row_global % row_block
    col_inner = col_global % col_block
    place = (col_inner // LANES) * row_block + row_inner
    low = (col_inner % LANES)[None, :]
    common = jnp.bitwise_count((row_global // row_block) & lax.axis_index("row"))
    common += jnp.bitwise_count((col_global // col_block) & lax.axis_index("col"))
    scale = 1.0 / math.sqrt(row_block * row_count * d_total * TOK_EX)
    weight = jnp.where(common % 2 == 0, scale, -scale).astype(jnp.float32)
    terms = sketch(hidden_all, grad_all, ids[:, None], sign_bits, place, low) * weight[None, :]
    return lax.psum_scatter(terms, ("row", "col"), scatter_dimension=1, tiled=True)


def solution(mesh):
    placed = (
        P(("groups", "col"), "row"),
        P(("groups", "row"), "col"),
        P(("groups", "col")),
        P("row", "col"),
        P(),
    )
    return jax.shard_map(
        shards, mesh=mesh, in_specs=placed, out_specs=P("groups", ("row", "col")), check_vma=False
    )
```

time: 1970 us -> 243 us (0.12)
  blocking collectives: 561 us -> 6.25 us
  waiting for transfers between devices: 676 us -> 149 us
  matrix products: 407 us -> 0 us
  local copies, waits for them, and re-layouts: 253 us -> 7.58 us
  Pallas kernels: 0 us -> 65 us
  other arithmetic: 30.1 us -> 1.68 us
    all_to_all x2 -> x0, blocking collectives: 555 us -> none  [the longest x1 367 us: shards(): lax.all_to_all(mixed, 'row', split_axis=1, concat_axis=3, tiled=True)]
    all_to_all x2 -> x0, waiting for transfers between devices: 546 us -> none  [the longest x1 363 us: shards(): lax.all_to_all(stacked, 'row', split_axis=3, concat_axis=1, tiled=True)]
    dot_general x5 -> x0, matrix products: 407 us -> none  [the longest x1 257 us: shards(): jnp.einsum('ij,ejk->eik', sylvester(row_block), flipped, precision=highest)]
    gather x1 -> x0, local copies, waits for them, and re-layouts: 91.4 us -> none  [shards(): terms = jnp.where(owner[None, :], jnp.take(whole, flat_inner, axis=1), 0.0)]
    all_to_all x4 -> x0, local copies, waits for them, and re-layouts: 74.5 us -> none  [the longest x2 42 us: shards(): lax.all_to_all(mixed, 'row', split_axis=1, concat_axis=3, tiled=True)]
    pallas_call x0 -> x1, Pallas kernels: none -> 65 us  [sketch(): pl.pallas_call(functools.partial(kernel, order), out_shape=jax.ShapeDtype...]
    transpose x2 -> x0, local copies, waits for them, and re-layouts: 25.9 us -> none  [the longest x1 17.7 us: shards(): jnp.einsum('ij,ejrc->eirc', col_table, lax.all_to_all(stacked, 'col', spl...]
    reshape x1 -> x0, local copies, waits for them, and re-layouts: 25.4 us -> none  [shards(): stacked = local.reshape(EXAMPLES, 1, row_block, col_block)]
  transfers between devices with their start and end apart: 5 -> 3, of which waited for: 5 -> 3; matrix products, arithmetic and copies ran while one was open for 1% -> 2% of each run, Pallas kernels for 0% -> 0%
where the time goes in v1:
time: 243 us; the launch traced here: 242 us
  waiting for transfers between devices  149 us (61%)
  Pallas kernels  65 us (27%)
  between operations  13.1 us (5%)
  local copies, waits for them, and re-layouts  7.58 us (3%)
  blocking collectives  6.25 us (3%)
    unnamed x4, waiting for transfers between devices  73.4 us
    pallas_call x1, Pallas kernels, sketch(): pl.pallas_call(functools.partial(kernel, order), out_shape=jax.ShapeDtype...  65 us
    all_gather x1, waiting for transfers between devices, shards(): grad_all = lax.all_gather(grad_out, 'row', axis=0, tiled=True)  39.9 us
    all_gather x1, waiting for transfers between devices, shards(): hidden_all = lax.all_gather(hidden.T, 'col', axis=1, tiled=True)  35.3 us
    unnamed x5, local copies, waits for them, and re-layouts  6.56 us
    all_gather x1, blocking collectives, shards(): ids = lax.all_gather(example_ids, 'col', axis=0, tiled=True)  6.25 us
  transfers between devices with their start and end apart: 3, of which 3 were waited for; matrix products, arithmetic and copies ran while one was open for 2% of the time, Pallas kernels for 0%

profile of v1, /device:TPU:0, one launch (start us, length us, event | category | flops | bytes accessed | tf_op | source)
XLA Modules:
  0.0 242.3 jit_solution(1925106627079446445)
XLA Ops:
  6.5 0.0 copy-start
  6.5 0.0 all-gather.6.cloned.1.call-start
  6.5 0.7 all-gather.6.cloned.1.call-update
  7.3 0.0 all-gather.4.cloned.1.call-start
  7.3 2.3 copy.11
  9.6 0.0 all-gather.4.cloned.1.call-update
  9.6 0.0 reduce-scatter.4.cloned.1.call-start
  9.7 6.3 %all-gather = s32[4,1,256]{2,1,0:T(1,128)S(1)} all-gather(s32[1,1,256]{2,1,0:T(1,128)} %bitcast.11), channel_id=1, replica_groups=mesh['groups'=2,'row'=4,'col'=4] {'col'}, dimensions={0}, use_global_device_ids=true | all-gather | bytes 5120 | tf_op jit(solution)/shard_map/all_gather | solution.py:170
  15.9 1.0 copy.12.ids_ref
  16.9 0.0 copy-done
  16.9 0.1 compare_select_fusion
  17.0 0.7 add_select_fusion.2
  17.7 39.9 %all-gather.6.cloned.1.call-done.grad_ref = bf16[1024,1024]{1,0:T(8,128)(2,1)} async-done(((bf16[256,1024]{1,0:T(8,128)(2,1)}), bf16[1024,1024]{1,0:T(8,128)(2,1)}) %all-gather.6.cloned.1.call-update) | async-done | bytes 2097168 | tf_op jit(solution)/shard_map/all_gather | solution.py:168
  57.6 35.3 %all-gather.4.cloned.1.call-done.hidden_ref = bf16[2048,1024]{1,0:T(8,128)(2,1)} async-done(((bf16[2048,256]{1,0:T(8,128)(2,1)}), bf16[2048,1024]{1,0:T(8,128)(2,1)}) %all-gather.4.cloned.1.call-update) | async-done | bytes 4194320 | tf_op jit(solution)/shard_map/all_gather | solution.py:169
  92.9 65.0 %sketch.1 = f32[2,8192]{1,0:T(2,128)} custom-call(s32[8192]{0:T(1024)} %get-tuple-element.6.place_ref, s32[1024,1]{1,0:T(8,128)} %copy.12.ids_ref, s32[1,8192]{1,0:T(1,128)} %bitcast.9, bf16[2048,1024]{1,0:T(8,128)(2,1)} %all-gather.4.cloned.1.call-done.hidden_ref, bf16[1024,1024]{1,0:T(8,128)(2,1)} %all-gather.6.cloned.1.call-done.grad_ref, ...), custom_call_target="tpu_custom_call" | custom-call | tf_op jit(solution)/shard_map/sketch/pallas_call | solution.py:134
  157.9 0.9 broadcast_multiply_fusion
  158.8 2.6 %copy.13 = f32[2,8192]{0,1:T(8,128)} copy(f32[2,8192]{1,0:T(2,128)S(1)} %broadcast_multiply_fusion) | data formatting | bytes 131072
  161.4 0.0 reduce-scatter.4.cloned.1.call-update
  161.4 72.6 %reduce-scatter.4.cloned.1.call-done = f32[512,2]{1,0:T(8,128)} async-done(((f32[8192,2]{1,0:T(8,128)}), f32[512,2]{1,0:T(8,128)}) %reduce-scatter.4.cloned.1.call-update) | async-done | bytes 4112
  234.1 1.7 copy.14
Async XLA Ops:
  6.5 10.4 %copy-start = (s32[8192]{0:T(1024)S(1)}, s32[8192]{0:T(1024)}, u32[]{:S(2)}) copy-start(s32[8192]{0:T(1024)} %param.11) | copy-start | bytes 98308
  6.5 51.1 %all-gather.6.cloned.1.call-start = ((), (), s32[]{:S(2)}) async-start(), calls=%async_computation.2 | async-start | bytes 2621440 | tf_op jit(solution)/shard_map/all_gather | solution.py:168
  7.3 85.7 %all-gather.4.cloned.1.call-start = ((), (), s32[]{:S(2)}) async-start(), calls=%async_computation.1 | async-start | bytes 5242880 | tf_op jit(solution)/shard_map/all_gather | solution.py:169
  9.6 224.5 %reduce-scatter.4.cloned.1.call-start = ((), (), s32[]{:S(2)}) async-start(), calls=%async_computation.3 | async-start | bytes 4456448
Sparse Core Ops, SparseCore 0:
  8.9 48.6 all-gather.5
  59.1 33.7 all-gather.3
  161.6 72.4 reduce-scatter.3

commit v2 on v1

--- a/solution.py
+++ b/solution.py
@@ -15,6 +15,8 @@
 WIDE = 256
 UNROLL = 16
 BATCH = 1024
+PIECES = 4
+MESH = pl.DeviceIdType.MESH
 
 
 def sylvester(order):
@@ -51,7 +53,7 @@
     chunks = table.shape[1]
     samples = low_ref.shape[1]
 
-    labels = ids_ref[...]
+    labels = jnp.concatenate([ids_ref[...]] * (WIDE // LANES), axis=1).astype(jnp.float32)
     for e in range(EXAMPLES):
         masked = jnp.where(labels == e, grad_ref[...].astype(jnp.float32), 0.0).astype(jnp.bfloat16)
 
@@ -138,7 +140,7 @@
             num_scalar_prefetch=1,
             grid=(columns // WIDE,),
             in_specs=[
-                pl.BlockSpec((tokens, 1), whole),
+                pl.BlockSpec((tokens, LANES), whole),
                 pl.BlockSpec((1, low.shape[1]), whole),
                 pl.BlockSpec((rows, tokens), whole),
                 pl.BlockSpec((tokens, WIDE), lambda j, place: (0, j)),
@@ -159,15 +161,212 @@
     )(place, ids, low, hidden, grad, sign_bits, jnp.concatenate([half, half], axis=1), sylvester(LANES))
 
 
+def gather_kernel(
+    rows, chips, hidden_ref, ids_ref, grad_ref, hidden_out, ids_out, grad_out,
+    own_sem, row_send, row_recv, chip_send, chip_recv, core_send, core_recv,
+):
+    me = lax.axis_index("row")
+    col = lax.axis_index("col")
+    chip, core = col // 2, col % 2
+    tokens = ids_ref.shape[0]
+    high = hidden_ref.shape[0] // PIECES
+    count = grad_ref.shape[0]
+    deep = count // PIECES
+
+    def row_copy(origin, piece, up):
+        at = pl.ds(pl.multiple_of(origin * count + piece * deep, deep), deep)
+        return pltpu.make_async_remote_copy(
+            src_ref=grad_out.at[at, :], dst_ref=grad_out.at[at, :],
+            send_sem=row_send.at[up, origin, piece], recv_sem=row_recv.at[origin, piece],
+            device_id={"row": me + 1 if up else me - 1}, device_id_type=MESH,
+        )
+
+    def row_first(piece, up):
+        at = pl.ds(pl.multiple_of(me * count + piece * deep, deep), deep)
+        return pltpu.make_async_remote_copy(
+            src_ref=grad_ref.at[pl.ds(piece * deep, deep), :], dst_ref=grad_out.at[at, :],
+            send_sem=row_send.at[up, me, piece], recv_sem=row_recv.at[me, piece],
+            device_id={"row": me + 1 if up else me - 1}, device_id_type=MESH,
+        )
+
+    def hidden_view(origin, piece):
+        if piece == PIECES:
+            return ids_out.at[pl.ds(pl.multiple_of(origin * tokens, tokens), tokens), :]
+        return hidden_out.at[pl.ds(piece * high, high), pl.ds(pl.multiple_of(origin * tokens, tokens), tokens)]
+
+    def hidden_copy(origin, piece, send, recv, target, own):
+        view = hidden_view(origin, piece)
+        source = view
+        if own:
+            source = ids_ref if piece == PIECES else hidden_ref.at[pl.ds(piece * high, high), :]
+        return pltpu.make_async_remote_copy(
+            src_ref=source, dst_ref=view, send_sem=send, recv_sem=recv.at[origin, piece],
+            device_id={"col": target}, device_id_type=MESH,
+        )
+
+    def chip_copy(origin_chip, piece, up, own=False):
+        origin = origin_chip * 2 + core
+        return hidden_copy(origin, piece, chip_send.at[up, origin, piece], chip_recv, col + 2 if up else col - 2, own)
+
+    def core_copy(origin, piece, own=False):
+        return hidden_copy(origin, piece, core_send.at[origin, piece], core_recv, chip * 2 + 1 - core, own)
+
+    sides = [
+        (me > 0, {"row": me - 1}), (me < rows - 1, {"row": me + 1}),
+        (chip > 0, {"col": col - 2}), (chip < chips - 1, {"col": col + 2}),
+        (core >= 0, {"col": chip * 2 + 1 - core}),
+    ]
+    barrier = pltpu.get_barrier_semaphore()
+    for there, target in sides:
+        @pl.when(there)
+        def _():
+            pl.semaphore_signal(barrier, inc=1, device_id=target, device_id_type=MESH)
+    pl.semaphore_wait(barrier, sum(there.astype(jnp.int32) for there, _ in sides))
+
+    kinds = [PIECES] + list(range(PIECES))
+    for piece in range(PIECES):
+        for up in (0, 1):
+            @pl.when(me < rows - 1 if up else me > 0)
+            def _():
+                row_first(piece, up).start()
+    for piece in kinds:
+        for up in (0, 1):
+            @pl.when(chip < chips - 1 if up else chip > 0)
+            def _():
+                chip_copy(chip, piece, up, own=True).start()
+        core_copy(col, piece, own=True).start()
+    mine = [
+        pltpu.make_async_copy(hidden_ref, hidden_out.at[:, pl.ds(pl.multiple_of(col * tokens, tokens), tokens)], own_sem.at[0]),
+        pltpu.make_async_copy(ids_ref, hidden_view(col, PIECES), own_sem.at[1]),
+        pltpu.make_async_copy(grad_ref, grad_out.at[pl.ds(pl.multiple_of(me * count, count), count), :], own_sem.at[2]),
+    ]
+    for copy in mine:
+        copy.start()
+
+    for far in range(1, max(rows, chips)):
+        for piece in kinds:
+            for up in (0, 1):
+                if far < rows and piece < PIECES:
+                    origin = me - far if up else me + far
+
+                    @pl.when(origin >= 0 if up else origin < rows)
+                    def _():
+                        row_copy(origin, piece, up).wait_recv()
+
+                        @pl.when(me < rows - 1 if up else me > 0)
+                        def _():
+                            row_copy(origin, piece, up).start()
+                if far < chips:
+                    source = chip - far if up else chip + far
+
+                    @pl.when(source >= 0 if up else source < chips)
+                    def _():
+                        chip_copy(source, piece, up).wait_recv()
+
+                        @pl.when(chip < chips - 1 if up else chip > 0)
+                        def _():
+                            chip_copy(source, piece, up).start()
+                        core_copy(source * 2 + core, piece).start()
+
+    for copy in mine:
+        copy.wait()
+    for place in range(chips):
+        for piece in kinds:
+            core_copy(place * 2 + 1 - core, piece).wait_recv()
+            core_copy(place * 2 + core, piece).wait_send()
+    for far in range(max(rows, chips)):
+        for piece in kinds:
+            for up in (0, 1):
+                if far < rows and piece < PIECES:
+                    origin = me - far if up else me + far
+
+                    @pl.when((origin >= 0) & (me < rows - 1) if up else (origin < rows) & (me > 0))
+                    def _():
+                        row_copy(origin, piece, up).wait_send()
+                if far < chips:
+                    source = chip - far if up else chip + far
+
+                    @pl.when((source >= 0) & (chip < chips - 1) if up else (source < chips) & (chip > 0))
+                    def _():
+                        chip_copy(source, piece, up).wait_send()
+
+
+def gather(hidden, ids, grad, rows, cols):
+    units, tokens = hidden.shape
+    shape = jax.ShapeDtypeStruct
+    anywhere = pl.BlockSpec(memory_space=pl.ANY)
+    dma = pltpu.SemaphoreType.DMA
+    return pl.pallas_call(
+        functools.partial(gather_kernel, rows, cols // 2),
+        out_shape=(
+            shape((units, tokens * cols), jnp.bfloat16),
+            shape((tokens * cols, LANES), jnp.bfloat16),
+            shape((grad.shape[0] * rows, grad.shape[1]), jnp.bfloat16),
+        ),
+        in_specs=[anywhere] * 3,
+        out_specs=[anywhere] * 3,
+        scratch_shapes=[
+            dma((3,)), dma((2, rows, PIECES)), dma((rows, PIECES)),
+            dma((2, cols, PIECES + 1)), dma((cols, PIECES + 1)),
+            dma((cols, PIECES + 1)), dma((cols, PIECES + 1)),
+        ],
+        compiler_params=pltpu.CompilerParams(collective_id=0, has_side_effects=True),
+        name="gather",
+    )(hidden, ids, grad)
+
+
+def reduce_kernel(rows, cols, terms_ref, out_ref, arrived, send_sem, recv_sem):
+    me = lax.axis_index("row") * cols + lax.axis_index("col")
+    count = rows * cols
+
+    def copy(t):
+        target = lax.rem(me + t, count)
+        return pltpu.make_async_remote_copy(
+            src_ref=terms_ref.at[target], dst_ref=arrived.at[me],
+            send_sem=send_sem.at[t], recv_sem=recv_sem.at[t],
+            device_id={"row": target // cols, "col": lax.rem(target, cols)}, device_id_type=MESH,
+        )
+
+    def greet(t, _):
+        target = lax.rem(me + t, count)
+        pl.semaphore_signal(
+            barrier, inc=1, device_id={"row": target // cols, "col": lax.rem(target, cols)}, device_id_type=MESH
+        )
+        return 0
+
+    barrier = pltpu.get_barrier_semaphore()
+    lax.fori_loop(1, count, greet, 0)
+    pl.semaphore_wait(barrier, count - 1)
+    lax.fori_loop(1, count, lambda t, _: (copy(t).start(), 0)[1], 0)
+    arrived[me] = terms_ref[me]
+    lax.fori_loop(1, count, lambda t, _: (copy(t).wait(), 0)[1], 0)
+    out_ref[...] = jnp.sum(arrived[...], axis=0)
+
+
+def reduce(terms, rows, cols):
+    return pl.pallas_call(
+        functools.partial(reduce_kernel, rows, cols),
+        out_shape=jax.ShapeDtypeStruct(terms.shape[1:], jnp.float32),
+        in_specs=[pl.BlockSpec(memory_space=pltpu.VMEM)],
+        out_specs=pl.BlockSpec(memory_space=pltpu.VMEM),
+        scratch_shapes=[
+            pltpu.VMEM(terms.shape, jnp.float32),
+            pltpu.SemaphoreType.DMA((rows * cols,)),
+            pltpu.SemaphoreType.DMA((rows * cols,)),
+        ],
+        compiler_params=pltpu.CompilerParams(collective_id=1, has_side_effects=True),
+        name="reduce",
+    )(terms)
+
+
 def shards(hidden, grad_out, example_ids, sign_bits, sample_index):
     row_block = hidden.shape[1]
     col_block = grad_out.shape[1]
     row_count = lax.axis_size("row")
     col_count = lax.axis_size("col")
     d_total = col_block * col_count
-    grad_all = lax.all_gather(grad_out, "row", axis=0, tiled=True)
-    hidden_all = lax.all_gather(hidden.T, "col", axis=1, tiled=True)
-    ids = lax.all_gather(example_ids, "col", axis=0, tiled=True)
+    labels = jnp.broadcast_to(example_ids[:, None], (hidden.shape[0], LANES)).astype(jnp.bfloat16)
+    hidden_all, ids, grad_all = gather(hidden.T, labels, grad_out, row_count, col_count)
     row_global = sample_index // d_total
     col_global = sample_index % d_total
     row_inner = row_global % row_block
@@ -178,8 +377,9 @@
     common += jnp.bitwise_count((col_global // col_block) & lax.axis_index("col"))
     scale = 1.0 / math.sqrt(row_block * row_count * d_total * TOK_EX)
     weight = jnp.where(common % 2 == 0, scale, -scale).astype(jnp.float32)
-    terms = sketch(hidden_all, grad_all, ids[:, None], sign_bits, place, low) * weight[None, :]
-    return lax.psum_scatter(terms, ("row", "col"), scatter_dimension=1, tiled=True)
+    terms = sketch(hidden_all, grad_all, ids, sign_bits, place, low) * weight[None, :]
+    terms = terms.reshape(EXAMPLES, row_count * col_count, -1).transpose(1, 0, 2)
+    return reduce(terms, row_count, col_count)
 
 
 def solution(mesh):

time: 243 us -> 137 us (0.56)
  waiting for transfers between devices: 149 us -> 0 us
  Pallas kernels: 65 us -> 128 us
  between operations: 13.1 us -> 0.02 us
  blocking collectives: 6.25 us -> 0 us
  local copies, waits for them, and re-layouts: 7.58 us -> 4.29 us
    all_gather x2 -> x0, waiting for transfers between devices: 75.2 us -> none  [the longest x1 39.9 us: shards(): grad_all = lax.all_gather(grad_out, 'row', axis=0, tiled=True)]
    unnamed x4 -> x0, waiting for transfers between devices: 73.4 us -> none
    pallas_call x0 -> x2, Pallas kernels: none -> 63.9 us  [the longest x1 55.2 us: gather(): pl.pallas_call(functools.partial(gather_kernel, rows, cols // 2), out_sha...]
    all_gather x1 -> x0, blocking collectives: 6.25 us -> none  [shards(): ids = lax.all_gather(example_ids, 'col', axis=0, tiled=True)]
    unnamed x5 -> x4, local copies, waits for them, and re-layouts: 6.56 us -> 3.55 us
  transfers between devices with their start and end apart: 3 -> 0, of which waited for: 3 -> 0; matrix products, arithmetic and copies ran while one was open for 2% -> 0% of each run, Pallas kernels for 0% -> 0%
where the time goes in v2:
time: 137 us; the launch traced here: 136 us
  Pallas kernels  128 us (93%)
  local copies, waits for them, and re-layouts  4.29 us (3%)
  other arithmetic  3.75 us (3%)
    pallas_call x1, Pallas kernels, sketch(): pl.pallas_call(functools.partial(kernel, order), out_shape=jax.ShapeDtype...  64.1 us
    pallas_call x1, Pallas kernels, gather(): pl.pallas_call(functools.partial(gather_kernel, rows, cols // 2), out_sha...  55.2 us
    pallas_call x1, Pallas kernels, reduce(): pl.pallas_call(functools.partial(reduce_kernel, rows, cols), out_shape=ja...  8.74 us
    unnamed x4, local copies, waits for them, and re-layouts  3.55 us

profile of v2, /device:TPU:0, one launch (start us, length us, event | category | flops | bytes accessed | tf_op | source)
XLA Modules:
  0.0 136.1 jit_solution(3521995196930066633)
XLA Ops:
  0.0 2.3 %copy.8 = bf16[256,2048]{0,1:T(8,128)(2,1)} copy(bf16[256,2048]{1,0:T(8,128)(2,1)} %param.7) | data formatting | bytes 2097152 | tf_op args[0]
  2.3 0.7 convert_element_type.12
  3.0 0.7 broadcast_in_dim.18.ids_ref
  3.7 55.2 %gather.1 = (bf16[2048,1024]{1,0:T(8,128)(2,1)}, bf16[1024,128]{1,0:T(8,128)(2,1)}, bf16[1024,1024]{1,0:T(8,128)(2,1)}) custom-call(bf16[2048,256]{1,0:T(8,128)(2,1)} %bitcast.5, bf16[256,128]{1,0:T(8,128)(2,1)} %broadcast_in_dim.18.ids_ref, bf16[256,1024]{1,0:T(8,128)(2,1)} %grad_ref.1), custom_call_target="tpu_custom_call" | custom-call | tf_op jit(solution)/shard_map/gather/pallas_call | solution.py:299
  58.9 1.5 %add_select_fusion.2 = (s32[8192]{0:T(1024)}, s32[8192]{0:T(1024)}) fusion(s32[8192]{0:T(1024)} %param.11), kind=kLoop, calls=%fused_computation.4 | loop fusion | flops 507904 | bytes 98304 | tf_op jit(solution)/shard_map/jit(remainder)/select_n | solution.py:375
  60.4 0.0 copy-start
  60.4 64.1 %sketch.1 = f32[2,8192]{1,0:T(2,128)} custom-call(s32[8192]{0:T(1024)} %get-tuple-element.12.place_ref, bf16[1024,128]{1,0:T(8,128)(2,1)} %get-tuple-element.8.ids_ref, s32[1,8192]{1,0:T(1,128)} %bitcast.7, bf16[2048,1024]{1,0:T(8,128)(2,1)} %get-tuple-element.9.hidden_ref, bf16[1024,1024]{1,0:T(8,128)(2,1)} %get-tuple-element.10.grad_ref, ...), custom_call_target="tpu_custom_call" | custom-call | tf_op jit(solution)/shard_map/sketch/pallas_call | solution.py:136
  124.5 0.0 copy-done
  124.5 0.1 compare_select_fusion
  124.6 1.5 %broadcast_multiply_fusion = f32[2,8192]{1,0:T(2,128)} fusion(f32[2,8192]{1,0:T(2,128)} %sketch.1, f32[8192]{0:T(1024)S(1)} %compare_select_fusion), kind=kLoop, calls=%fused_computation.30 | loop fusion | flops 16384 | bytes 163840 | tf_op jit(solution)/shard_map/mul | solution.py:380
  126.1 8.7 %reduce.1 = f32[2,512]{1,0:T(2,128)} custom-call(f32[16,2,512]{2,1,0:T(2,128)} %bitcast.6), custom_call_target="tpu_custom_call" | custom-call | tf_op jit(solution)/shard_map/reduce/pallas_call | solution.py:347
  134.9 1.3 copy.10
Async XLA Ops:
  60.4 64.1 %copy-start = (s32[8192]{0:T(1024)S(1)}, s32[8192]{0:T(1024)}, u32[]{:S(2)}) copy-start(s32[8192]{0:T(1024)} %param.11) | copy-start | bytes 98308

commit v3 on v2

--- a/solution.py
+++ b/solution.py
@@ -16,6 +16,8 @@
 UNROLL = 16
 BATCH = 1024
 PIECES = 4
+GROUP = 4
+FUSED = 4
 MESH = pl.DeviceIdType.MESH
 
 
@@ -43,61 +45,26 @@
     return high, (values - high.astype(jnp.float32)).astype(jnp.bfloat16)
 
 
-def kernel(
-    order, place_ref, ids_ref, low_ref, hidden_ref, grad_ref, sign_ref, pair_ref, lane_ref,
-    out_ref, table, flipped, parts, picked,
-):
+def sample_kernel(place_ref, low_ref, mixed_ref, lane_ref, out_ref, table, picked):
     step = pl.program_id(0)
-    rows = hidden_ref.shape[0]
-    blocks = rows // order
-    chunks = table.shape[1]
+    chunks, tile = mixed_ref.shape[1:3]
+    rows = table.shape[2]
+    tiles = rows // tile
+    example, start = step // tiles, (step % tiles) * tile
     samples = low_ref.shape[1]
 
-    labels = jnp.concatenate([ids_ref[...]] * (WIDE // LANES), axis=1).astype(jnp.float32)
-    for e in range(EXAMPLES):
-        masked = jnp.where(labels == e, grad_ref[...].astype(jnp.float32), 0.0).astype(jnp.bfloat16)
-
-        def multiply(b, _):
-            at = pl.ds(pl.multiple_of(b * order, order), order)
-            grads = jnp.dot(hidden_ref[at, :], masked, preferred_element_type=jnp.float32)
-            flipped[b] = jnp.where(sign_ref[at, :] == 0, grads, -grads)
-            return 0
-
-        lax.fori_loop(0, blocks, multiply, 0)
-
-        def mix(i, _):
-            at = pl.ds(pl.multiple_of(i * 16, 16), 16)
-            below = pl.ds(pl.multiple_of(order + i * 16, 16), 16)
-            values = butterfly([flipped[b, at, :] for b in range(blocks)])
-            for b in range(blocks):
-                high, low = split(values[b])
-                parts[b, at, :] = high
-                parts[b, below, :] = low
-            return 0
-
-        lax.fori_loop(0, order // 16, mix, 0)
-
-        def transform(b, _):
-            at = pl.ds(pl.multiple_of(b * order, order), order)
-            values = jnp.dot(pair_ref[...], parts[b], preferred_element_type=jnp.float32)
-            for half in range(WIDE // LANES):
-                table[e, step * (WIDE // LANES) + half, at, :] = values[:, half * LANES:(half + 1) * LANES]
-            return 0
-
-        lax.fori_loop(0, blocks, transform, 0)
+    def across(i, _):
+        at = pl.ds(pl.multiple_of(i * 16, 16), 16)
+        to = pl.ds(pl.multiple_of(start + i * 16, 16), 16)
+        values = butterfly([mixed_ref[0, c, at, :] for c in range(chunks)])
+        for c in range(chunks):
+            table[example, c, to, :] = values[c]
+        return 0
+
+    lax.fori_loop(0, tile // 16, across, 0)
 
     @pl.when(step == pl.num_programs(0) - 1)
     def _():
-        for e in range(EXAMPLES):
-            def across(i, _):
-                at = pl.ds(pl.multiple_of(i * 16, 16), 16)
-                values = butterfly([table[e, c, at, :] for c in range(chunks)])
-                for c in range(chunks):
-                    table[e, c, at, :] = values[c]
-                return 0
-
-            lax.fori_loop(0, rows // 16, across, 0)
-
         flat = table.reshape(EXAMPLES, chunks * rows, LANES)
         lane = lax.broadcasted_iota(jnp.int32, (LANES, BATCH), 0)
 
@@ -126,44 +93,35 @@
         lax.fori_loop(0, samples // BATCH, sample, 0)
 
 
-def sketch(hidden, grad, ids, sign_bits, place, low):
-    rows, tokens = hidden.shape
-    columns = grad.shape[1]
-    order = min(rows, 256)
-    chunks = columns // LANES
+def sample(mixed, place, low):
+    _, chunks, rows, _ = mixed.shape
+    tile = min(rows, 512)
     whole = lambda j, place: (0, 0)
-    half = sylvester(order)
     return pl.pallas_call(
-        functools.partial(kernel, order),
+        sample_kernel,
         out_shape=jax.ShapeDtypeStruct((EXAMPLES, low.shape[1]), jnp.float32),
         grid_spec=pltpu.PrefetchScalarGridSpec(
             num_scalar_prefetch=1,
-            grid=(columns // WIDE,),
+            grid=(EXAMPLES * (rows // tile),),
             in_specs=[
-                pl.BlockSpec((tokens, LANES), whole),
                 pl.BlockSpec((1, low.shape[1]), whole),
-                pl.BlockSpec((rows, tokens), whole),
-                pl.BlockSpec((tokens, WIDE), lambda j, place: (0, j)),
-                pl.BlockSpec((rows, WIDE), lambda j, place: (0, j)),
-                pl.BlockSpec((order, 2 * order), whole),
+                pl.BlockSpec((1, chunks, tile, LANES), lambda j, place: (j // (rows // tile), 0, j % (rows // tile), 0)),
                 pl.BlockSpec((LANES, LANES), whole),
             ],
             out_specs=pl.BlockSpec((EXAMPLES, low.shape[1]), whole),
             scratch_shapes=[
                 pltpu.VMEM((EXAMPLES, chunks, rows, LANES), jnp.float32),
-                pltpu.VMEM((rows // order, order, WIDE), jnp.float32),
-                pltpu.VMEM((rows // order, 2 * order, WIDE), jnp.bfloat16),
                 pltpu.VMEM((EXAMPLES, BATCH, LANES), jnp.float32),
             ],
         ),
         compiler_params=pltpu.CompilerParams(vmem_limit_bytes=56 << 20),
-        name="sketch",
-    )(place, ids, low, hidden, grad, sign_bits, jnp.concatenate([half, half], axis=1), sylvester(LANES))
+        name="sample",
+    )(place, low, mixed, sylvester(LANES))
 
 
 def gather_kernel(
-    rows, chips, hidden_ref, ids_ref, grad_ref, hidden_out, ids_out, grad_out,
-    own_sem, row_send, row_recv, chip_send, chip_recv, core_send, core_recv,
+    rows, chips, order, hidden_ref, ids_ref, grad_ref, sign_ref, pair_ref, mixed_ref,
+    hidden_out, ids_out, grad_out, signs, flipped, parts, staged, sign_sem, out_sem, own_sem, row_send, row_recv, chip_send, chip_recv, core_send, core_recv,
 ):
     me = lax.axis_index("row")
     col = lax.axis_index("col")
@@ -171,20 +129,23 @@
     tokens = ids_ref.shape[0]
     high = hidden_ref.shape[0] // PIECES
     count = grad_ref.shape[0]
-    deep = count // PIECES
+    units = hidden_ref.shape[0]
+    steps = grad_ref.shape[1] // WIDE
+    halves = WIDE // LANES
+    blocks = units // order
 
     def row_copy(origin, piece, up):
-        at = pl.ds(pl.multiple_of(origin * count + piece * deep, deep), deep)
+        view = grad_out.at[pl.ds(pl.multiple_of(origin * count, count), count), pl.ds(piece * WIDE, WIDE)]
         return pltpu.make_async_remote_copy(
-            src_ref=grad_out.at[at, :], dst_ref=grad_out.at[at, :],
+            src_ref=view, dst_ref=view,
             send_sem=row_send.at[up, origin, piece], recv_sem=row_recv.at[origin, piece],
             device_id={"row": me + 1 if up else me - 1}, device_id_type=MESH,
         )
 
     def row_first(piece, up):
-        at = pl.ds(pl.multiple_of(me * count + piece * deep, deep), deep)
+        wide = pl.ds(piece * WIDE, WIDE)
         return pltpu.make_async_remote_copy(
-            src_ref=grad_ref.at[pl.ds(piece * deep, deep), :], dst_ref=grad_out.at[at, :],
+            src_ref=grad_ref.at[:, wide], dst_ref=grad_out.at[pl.ds(pl.multiple_of(me * count, count), count), wide],
             send_sem=row_send.at[up, me, piece], recv_sem=row_recv.at[me, piece],
             device_id={"row": me + 1 if up else me - 1}, device_id_type=MESH,
         )
@@ -224,7 +185,7 @@
     pl.semaphore_wait(barrier, sum(there.astype(jnp.int32) for there, _ in sides))
 
     kinds = [PIECES] + list(range(PIECES))
-    for piece in range(PIECES):
+    for piece in range(steps):
         for up in (0, 1):
             @pl.when(me < rows - 1 if up else me > 0)
             def _():
@@ -243,10 +204,17 @@
     for copy in mine:
         copy.start()
 
+    def sign_copy(step):
+        wide = pl.ds(step * WIDE, WIDE)
+        return pltpu.make_async_copy(sign_ref.at[:, wide], signs.at[:, wide], sign_sem.at[step])
+
+    for step in range(steps):
+        sign_copy(step).start()
+
     for far in range(1, max(rows, chips)):
         for piece in kinds:
             for up in (0, 1):
-                if far < rows and piece < PIECES:
+                if far < rows - 1 and piece < steps:
                     origin = me - far if up else me + far
 
                     @pl.when(origin >= 0 if up else origin < rows)
@@ -273,11 +241,74 @@
     for place in range(chips):
         for piece in kinds:
             core_copy(place * 2 + 1 - core, piece).wait_recv()
+
+    def out_copy(step, e):
+        return pltpu.make_async_copy(
+            staged.at[step % 2, e], mixed_ref.at[e, pl.ds(step * halves, halves)], out_sem.at[step % 2, e]
+        )
+
+    for step in range(steps):
+        far = rows - 1
+        for up in (0, 1):
+            origin = me - far if up else me + far
+
+            @pl.when(origin >= 0 if up else origin < rows)
+            def _():
+                row_copy(origin, step, up).wait_recv()
+        sign_copy(step).wait()
+        wide = pl.ds(step * WIDE, WIDE)
+        labels = jnp.concatenate([ids_out[...]] * halves, axis=1).astype(jnp.float32)
+        for e in range(EXAMPLES):
+            masked = jnp.where(labels == e, grad_out[:, wide].astype(jnp.float32), 0.0).astype(jnp.bfloat16)
+            group = min(blocks, GROUP)
+
+            def multiply(b, _):
+                at = pl.ds(pl.multiple_of(b * group * order, group * order), group * order)
+                grads = jnp.dot(hidden_out[at, :], masked, preferred_element_type=jnp.float32)
+                flipped[at, :] = jnp.where(signs[at, wide] == 0, grads, -grads)
+                return 0
+
+            lax.fori_loop(0, blocks // group, multiply, 0)
+
+            def mix(i, _):
+                values = butterfly([
+                    flipped[pl.ds(pl.multiple_of(b * order + i * 16, 16), 16), :] for b in range(blocks)
+                ])
+                at = pl.ds(pl.multiple_of(i * 16, 16), 16)
+                below = pl.ds(pl.multiple_of(order + i * 16, 16), 16)
+                for b in range(blocks):
+                    high, low = split(values[b])
+                    parts[b, at, :] = high
+                    parts[b, below, :] = low
+                return 0
+
+            lax.fori_loop(0, order // 16, mix, 0)
+            if step >= 2:
+                out_copy(step - 2, e).wait()
+            fused = min(blocks, FUSED)
+
+            def transform(i, _):
+                for u in range(fused):
+                    b = i * fused + u
+                    at = pl.ds(pl.multiple_of(b * order, order), order)
+                    values = jnp.dot(pair_ref[...], parts[b], preferred_element_type=jnp.float32)
+                    for half in range(halves):
+                        staged[step % 2, e, half, at, :] = values[:, half * LANES:(half + 1) * LANES]
+                return 0
+
+            lax.fori_loop(0, blocks // fused, transform, 0)
+            out_copy(step, e).start()
+    for step in range(max(0, steps - 2), steps):
+        for e in range(EXAMPLES):
+            out_copy(step, e).wait()
+
+    for place in range(chips):
+        for piece in kinds:
             core_copy(place * 2 + core, piece).wait_send()
     for far in range(max(rows, chips)):
         for piece in kinds:
             for up in (0, 1):
-                if far < rows and piece < PIECES:
+                if far < rows and piece < steps:
                     origin = me - far if up else me + far
 
                     @pl.when((origin >= 0) & (me < rows - 1) if up else (origin < rows) & (me > 0))
@@ -291,28 +322,35 @@
                         chip_copy(source, piece, up).wait_send()
 
 
-def gather(hidden, ids, grad, rows, cols):
+def mix_rows(hidden, ids, grad, sign_bits, rows, cols):
     units, tokens = hidden.shape
-    shape = jax.ShapeDtypeStruct
+    depth, columns = tokens * cols, grad.shape[1]
+    order = min(units, 256)
+    half = sylvester(order)
     anywhere = pl.BlockSpec(memory_space=pl.ANY)
+    inside = pl.BlockSpec(memory_space=pltpu.VMEM)
     dma = pltpu.SemaphoreType.DMA
     return pl.pallas_call(
-        functools.partial(gather_kernel, rows, cols // 2),
-        out_shape=(
-            shape((units, tokens * cols), jnp.bfloat16),
-            shape((tokens * cols, LANES), jnp.bfloat16),
-            shape((grad.shape[0] * rows, grad.shape[1]), jnp.bfloat16),
-        ),
-        in_specs=[anywhere] * 3,
-        out_specs=[anywhere] * 3,
+        functools.partial(gather_kernel, rows, cols // 2, order),
+        out_shape=jax.ShapeDtypeStruct((EXAMPLES, columns // LANES, units, LANES), jnp.float32),
+        in_specs=[inside, inside, inside, anywhere, inside],
+        out_specs=anywhere,
         scratch_shapes=[
-            dma((3,)), dma((2, rows, PIECES)), dma((rows, PIECES)),
+            pltpu.VMEM((units, depth), jnp.bfloat16),
+            pltpu.VMEM((depth, LANES), jnp.bfloat16),
+            pltpu.VMEM((depth, columns), jnp.bfloat16),
+            pltpu.VMEM((units, columns), jnp.int32),
+            pltpu.VMEM((units, WIDE), jnp.float32),
+            pltpu.VMEM((units // order, 2 * order, WIDE), jnp.bfloat16),
+            pltpu.VMEM((2, EXAMPLES, WIDE // LANES, units, LANES), jnp.float32),
+            dma((columns // WIDE,)), dma((2, EXAMPLES)),
+            dma((3,)), dma((2, rows, columns // WIDE)), dma((rows, columns // WIDE)),
             dma((2, cols, PIECES + 1)), dma((cols, PIECES + 1)),
             dma((cols, PIECES + 1)), dma((cols, PIECES + 1)),
         ],
-        compiler_params=pltpu.CompilerParams(collective_id=0, has_side_effects=True),
-        name="gather",
-    )(hidden, ids, grad)
+        compiler_params=pltpu.CompilerParams(collective_id=0, has_side_effects=True, vmem_limit_bytes=56 << 20),
+        name="mix_rows",
+    )(hidden, ids, grad, sign_bits, jnp.concatenate([half, half], axis=1))
 
 
 def reduce_kernel(rows, cols, terms_ref, out_ref, arrived, send_sem, recv_sem):
@@ -366,7 +404,7 @@
     col_count = lax.axis_size("col")
     d_total = col_block * col_count
     labels = jnp.broadcast_to(example_ids[:, None], (hidden.shape[0], LANES)).astype(jnp.bfloat16)
-    hidden_all, ids, grad_all = gather(hidden.T, labels, grad_out, row_count, col_count)
+    mixed = mix_rows(hidden.T, labels, grad_out, sign_bits, row_count, col_count)
     row_global = sample_index // d_total
     col_global = sample_index % d_total
     row_inner = row_global % row_block
@@ -377,7 +415,7 @@
     common += jnp.bitwise_count((col_global // col_block) & lax.axis_index("col"))
     scale = 1.0 / math.sqrt(row_block * row_count * d_total * TOK_EX)
     weight = jnp.where(common % 2 == 0, scale, -scale).astype(jnp.float32)
-    terms = sketch(hidden_all, grad_all, ids, sign_bits, place, low) * weight[None, :]
+    terms = sample(mixed, place, low) * weight[None, :]
     terms = terms.reshape(EXAMPLES, row_count * col_count, -1).transpose(1, 0, 2)
     return reduce(terms, row_count, col_count)
 

time: 137 us -> 108 us (0.79)
  Pallas kernels: 128 us -> 99.5 us
    pallas_call x2, Pallas kernels: 119 us -> 89 us  [the longest x1 62.8 us: mix_rows(): pl.pallas_call(functools.partial(gather_kernel, rows, cols // 2, order),...]
    pallas_call x1, Pallas kernels: 8.74 us -> 10.5 us  [reduce(): pl.pallas_call(functools.partial(reduce_kernel, rows, cols), out_shape=ja...]
where the time goes in v3:
time: 108 us; the launch traced here: 107 us
  Pallas kernels  99.5 us (92%)
  local copies, waits for them, and re-layouts  4.26 us (4%)
  other arithmetic  3.73 us (3%)
    pallas_call x1, Pallas kernels, mix_rows(): pl.pallas_call(functools.partial(gather_kernel, rows, cols // 2, order),...  62.8 us
    pallas_call x1, Pallas kernels, sample(): pl.pallas_call(sample_kernel, out_shape=jax.ShapeDtypeStruct((EXAMPLES, l...  26.2 us
    pallas_call x1, Pallas kernels, reduce(): pl.pallas_call(functools.partial(reduce_kernel, rows, cols), out_shape=ja...  10.5 us
    unnamed x4, local copies, waits for them, and re-layouts  3.52 us

profile of v3, /device:TPU:0, one launch (start us, length us, event | category | flops | bytes accessed | tf_op | source)
XLA Modules:
  0.0 107.5 jit_solution(10471666517747847555)
XLA Ops:
  0.0 1.5 %add_select_fusion.2 = (s32[8192]{0:T(1024)}, s32[8192]{0:T(1024)}) fusion(s32[8192]{0:T(1024)} %param.11), kind=kLoop, calls=%fused_computation.4 | loop fusion | flops 507904 | bytes 98304 | tf_op jit(solution)/shard_map/jit(remainder)/select_n | solution.py:413
  1.5 2.3 %copy.8 = bf16[256,2048]{0,1:T(8,128)(2,1)} copy(bf16[256,2048]{1,0:T(8,128)(2,1)} %param.7) | data formatting | bytes 2097152 | tf_op args[0]
  3.7 0.7 convert_element_type.12
  4.4 0.7 broadcast_in_dim.19.ids_ref
  5.1 0.0 copy-start
  5.1 62.8 %mix_rows.1.mixed_ref = f32[2,8,2048,128]{3,2,1,0:T(8,128)} custom-call(bf16[2048,256]{1,0:T(8,128)(2,1)} %bitcast.5, bf16[256,128]{1,0:T(8,128)(2,1)} %broadcast_in_dim.19.ids_ref, bf16[256,1024]{1,0:T(8,128)(2,1)} %grad_ref.1, s32[2048,1024]{1,0:T(8,128)} %sign_ref.1, bf16[256,512]{1,0:T(8,128)(2,1)} %constant.122.pair_ref), custom_call_target="tpu_custom_call" | custom-call | tf_op jit(solution)/shard_map/mix_rows/pallas_call | solution.py:333
  67.9 26.2 %sample.1 = f32[2,8192]{1,0:T(2,128)} custom-call(s32[8192]{0:T(1024)} %get-tuple-element.6.place_ref, s32[1,8192]{1,0:T(1,128)} %bitcast.7, f32[2,8,2048,128]{3,2,1,0:T(8,128)} %mix_rows.1.mixed_ref, bf16[128,128]{1,0:T(8,128)(2,1)} %constant.121.clone.lane_ref), custom_call_target="tpu_custom_call" | custom-call | tf_op jit(solution)/shard_map/sample/pallas_call | solution.py:100
  94.1 0.0 copy-done
  94.1 0.1 compare_select_fusion
  94.2 1.5 %broadcast_multiply_fusion = f32[2,8192]{1,0:T(2,128)} fusion(f32[2,8192]{1,0:T(2,128)} %sample.1, f32[8192]{0:T(1024)S(1)} %compare_select_fusion), kind=kLoop, calls=%fused_computation.30 | loop fusion | flops 16384 | bytes 163840 | tf_op jit(solution)/shard_map/mul | solution.py:418
  95.7 10.5 %reduce.1 = f32[2,512]{1,0:T(2,128)} custom-call(f32[16,2,512]{2,1,0:T(2,128)} %bitcast.6), custom_call_target="tpu_custom_call" | custom-call | tf_op jit(solution)/shard_map/reduce/pallas_call | solution.py:385
  106.2 1.3 %copy.10 = f32[2,512]{1,0:T(2,128)} copy(f32[2,512]{1,0:T(2,128)} %reduce.1) | data formatting | bytes 8192
Async XLA Ops:
  5.1 89.0 %copy-start = (s32[8192]{0:T(1024)S(1)}, s32[8192]{0:T(1024)}, u32[]{:S(2)}) copy-start(s32[8192]{0:T(1024)} %param.11) | copy-start | bytes 98308

commit v4 on v3

--- a/solution.py
+++ b/solution.py
@@ -16,8 +16,8 @@
 UNROLL = 16
 BATCH = 1024
 PIECES = 4
-GROUP = 4
-FUSED = 4
+GROUP = 8
+FUSED = 8
 MESH = pl.DeviceIdType.MESH
 
 
@@ -120,8 +120,8 @@
 
 
 def gather_kernel(
-    rows, chips, order, hidden_ref, ids_ref, grad_ref, sign_ref, pair_ref, mixed_ref,
-    hidden_out, ids_out, grad_out, signs, flipped, parts, staged, sign_sem, out_sem, own_sem, row_send, row_recv, chip_send, chip_recv, core_send, core_recv,
+    rows, chips, order, given_ref, labels_ref, grad_ref, sign_ref, pair_ref, mixed_ref,
+    hidden_ref, ids_ref, hidden_out, ids_out, grad_out, signs, flipped, parts, staged, sign_sem, out_sem, own_sem, row_send, row_recv, chip_send, chip_recv, core_send, core_recv,
 ):
     me = lax.axis_index("row")
     col = lax.axis_index("col")
@@ -190,7 +190,11 @@
             @pl.when(me < rows - 1 if up else me > 0)
             def _():
                 row_first(piece, up).start()
+    ids_ref[...] = jnp.broadcast_to(labels_ref[...].astype(jnp.float32), (LANES, tokens)).T.astype(jnp.bfloat16)
     for piece in kinds:
+        if piece < PIECES:
+            part = given_ref[:, piece * high:(piece + 1) * high].astype(jnp.float32)
+            hidden_ref[piece * high:(piece + 1) * high, :] = part.T.astype(jnp.bfloat16)
         for up in (0, 1):
             @pl.when(chip < chips - 1 if up else chip > 0)
             def _():
@@ -323,7 +327,7 @@
 
 
 def mix_rows(hidden, ids, grad, sign_bits, rows, cols):
-    units, tokens = hidden.shape
+    tokens, units = hidden.shape
     depth, columns = tokens * cols, grad.shape[1]
     order = min(units, 256)
     half = sylvester(order)
@@ -336,6 +340,8 @@
         in_specs=[inside, inside, inside, anywhere, inside],
         out_specs=anywhere,
         scratch_shapes=[
+            pltpu.VMEM((units, tokens), jnp.bfloat16),
+            pltpu.VMEM((tokens, LANES), jnp.bfloat16),
             pltpu.VMEM((units, depth), jnp.bfloat16),
             pltpu.VMEM((depth, LANES), jnp.bfloat16),
             pltpu.VMEM((depth, columns), jnp.bfloat16),
@@ -403,8 +409,7 @@
     row_count = lax.axis_size("row")
     col_count = lax.axis_size("col")
     d_total = col_block * col_count
-    labels = jnp.broadcast_to(example_ids[:, None], (hidden.shape[0], LANES)).astype(jnp.bfloat16)
-    mixed = mix_rows(hidden.T, labels, grad_out, sign_bits, row_count, col_count)
+    mixed = mix_rows(hidden, example_ids[None, :], grad_out, sign_bits, row_count, col_count)
     row_global = sample_index // d_total
     col_global = sample_index % d_total
     row_inner = row_global % row_block

time: 108 us -> 114 us (1.056)
  Pallas kernels: 99.5 us -> 109 us
  local copies, waits for them, and re-layouts: 4.26 us -> 1.27 us
    pallas_call x1, Pallas kernels: 62.8 us -> 72.5 us  [mix_rows(): pl.pallas_call(functools.partial(gather_kernel, rows, cols // 2, order),...]
    unnamed x4 -> x3, local copies, waits for them, and re-layouts: 3.52 us -> 1.27 us
where the time goes in v4:
time: 114 us
  Pallas kernels  109 us (96%)
  other arithmetic  3.06 us (3%)
  local copies, waits for them, and re-layouts  1.27 us (1%)
    pallas_call x1, Pallas kernels, mix_rows(): pl.pallas_call(functools.partial(gather_kernel, rows, cols // 2, order),...  72.5 us
    pallas_call x1, Pallas kernels, sample(): pl.pallas_call(sample_kernel, out_shape=jax.ShapeDtypeStruct((EXAMPLES, l...  26.2 us
    pallas_call x1, Pallas kernels, reduce(): pl.pallas_call(functools.partial(reduce_kernel, rows, cols), out_shape=ja...  10.5 us

profile of v4, /device:TPU:0, one launch (start us, length us, event | category | flops | bytes accessed | tf_op | source)
XLA Modules:
  0.0 113.5 jit_solution(16817830887585168146)
XLA Ops:
  0.0 1.5 %add_select_fusion.2 = (s32[8192]{0:T(1024)}, s32[8192]{0:T(1024)}) fusion(s32[8192]{0:T(1024)} %param.11), kind=kLoop, calls=%fused_computation.4 | loop fusion | flops 507904 | bytes 98304 | tf_op jit(solution)/shard_map/jit(remainder)/select_n | solution.py:418
  1.5 0.0 copy-start
  1.5 72.5 %mix_rows.1.mixed_ref = f32[2,8,2048,128]{3,2,1,0:T(8,128)} custom-call(bf16[256,2048]{1,0:T(8,128)(2,1)} %given_ref.1, s32[1,256]{1,0:T(1,128)} %bitcast.7, bf16[256,1024]{1,0:T(8,128)(2,1)} %grad_ref.1, s32[2048,1024]{1,0:T(8,128)} %sign_ref.1, bf16[256,512]{1,0:T(8,128)(2,1)} %constant.122.pair_ref), custom_call_target="tpu_custom_call" | custom-call | tf_op jit(solution)/shard_map/mix_rows/pallas_call | solution.py:337
  73.9 26.2 %sample.1 = f32[2,8192]{1,0:T(2,128)} custom-call(s32[8192]{0:T(1024)} %get-tuple-element.6.place_ref, s32[1,8192]{1,0:T(1,128)} %bitcast.6, f32[2,8,2048,128]{3,2,1,0:T(8,128)} %mix_rows.1.mixed_ref, bf16[128,128]{1,0:T(8,128)(2,1)} %constant.121.clone.lane_ref), custom_call_target="tpu_custom_call" | custom-call | tf_op jit(solution)/shard_map/sample/pallas_call | solution.py:100
  100.2 0.0 copy-done
  100.2 0.1 compare_select_fusion
  100.3 1.5 %broadcast_multiply_fusion = f32[2,8192]{1,0:T(2,128)} fusion(f32[2,8192]{1,0:T(2,128)} %sample.1, f32[8192]{0:T(1024)S(1)} %compare_select_fusion), kind=kLoop, calls=%fused_computation.30 | loop fusion | flops 16384 | bytes 163840 | tf_op jit(solution)/shard_map/mul | solution.py:423
  101.8 10.5 %reduce.1 = f32[2,512]{1,0:T(2,128)} custom-call(f32[16,2,512]{2,1,0:T(2,128)} %bitcast.5), custom_call_target="tpu_custom_call" | custom-call | tf_op jit(solution)/shard_map/reduce/pallas_call | solution.py:391
  112.3 1.3 %copy.9 = f32[2,512]{1,0:T(2,128)} copy(f32[2,512]{1,0:T(2,128)} %reduce.1) | data formatting | bytes 8192
Async XLA Ops:
  1.5 98.7 %copy-start = (s32[8192]{0:T(1024)S(1)}, s32[8192]{0:T(1024)}, u32[]{:S(2)}) copy-start(s32[8192]{0:T(1024)} %param.11) | copy-start | bytes 98308

commit v5 on v3

--- a/solution.py
+++ b/solution.py
@@ -16,7 +16,7 @@
 UNROLL = 16
 BATCH = 1024
 PIECES = 4
-GROUP = 4
+GROUP = 8
 FUSED = 4
 MESH = pl.DeviceIdType.MESH
 
@@ -185,16 +185,17 @@
     pl.semaphore_wait(barrier, sum(there.astype(jnp.int32) for there, _ in sides))
 
     kinds = [PIECES] + list(range(PIECES))
+    for piece in kinds:
+        for up in (0, 1):
+            @pl.when(chip < chips - 1 if up else chip > 0)
+            def _():
+                chip_copy(chip, piece, up, own=True).start()
     for piece in range(steps):
         for up in (0, 1):
             @pl.when(me < rows - 1 if up else me > 0)
             def _():
                 row_first(piece, up).start()
     for piece in kinds:
-        for up in (0, 1):
-            @pl.when(chip < chips - 1 if up else chip > 0)
-            def _():
-                chip_copy(chip, piece, up, own=True).start()
         core_copy(col, piece, own=True).start()
     mine = [
         pltpu.make_async_copy(hidden_ref, hidden_out.at[:, pl.ds(pl.multiple_of(col * tokens, tokens), tokens)], own_sem.at[0]),

time: 108 us -> 107 us (level)
  Pallas kernels: 99.5 us -> 98 us
    pallas_call x1, Pallas kernels: 62.8 us -> 61.3 us  [mix_rows(): pl.pallas_call(functools.partial(gather_kernel, rows, cols // 2, order),...]
where the time goes in v5:
time: 107 us; the launch traced here: 106 us
  Pallas kernels  98 us (92%)
  local copies, waits for them, and re-layouts  4.26 us (4%)
  other arithmetic  3.73 us (3%)
    pallas_call x1, Pallas kernels, mix_rows(): pl.pallas_call(functools.partial(gather_kernel, rows, cols // 2, order),...  61.3 us
    pallas_call x1, Pallas kernels, sample(): pl.pallas_call(sample_kernel, out_shape=jax.ShapeDtypeStruct((EXAMPLES, l...  26.2 us
    pallas_call x1, Pallas kernels, reduce(): pl.pallas_call(functools.partial(reduce_kernel, rows, cols), out_shape=ja...  10.5 us
    unnamed x4, local copies, waits for them, and re-layouts  3.52 us

profile of v5, /device:TPU:0, one launch (start us, length us, event | category | flops | bytes accessed | tf_op | source)
XLA Modules:
  0.0 106.0 jit_solution(3726934642291947192)
XLA Ops:
  0.0 1.5 %add_select_fusion.2 = (s32[8192]{0:T(1024)}, s32[8192]{0:T(1024)}) fusion(s32[8192]{0:T(1024)} %param.11), kind=kLoop, calls=%fused_computation.4 | loop fusion | flops 507904 | bytes 98304 | tf_op jit(solution)/shard_map/jit(remainder)/select_n | solution.py:414
  1.5 2.3 %copy.8 = bf16[256,2048]{0,1:T(8,128)(2,1)} copy(bf16[256,2048]{1,0:T(8,128)(2,1)} %param.7) | data formatting | bytes 2097152 | tf_op args[0]
  3.7 0.7 convert_element_type.12
  4.4 0.7 broadcast_in_dim.19.ids_ref
  5.1 0.0 copy-start
  5.1 61.3 %mix_rows.1.mixed_ref = f32[2,8,2048,128]{3,2,1,0:T(8,128)} custom-call(bf16[2048,256]{1,0:T(8,128)(2,1)} %bitcast.5, bf16[256,128]{1,0:T(8,128)(2,1)} %broadcast_in_dim.19.ids_ref, bf16[256,1024]{1,0:T(8,128)(2,1)} %grad_ref.1, s32[2048,1024]{1,0:T(8,128)} %sign_ref.1, bf16[256,512]{1,0:T(8,128)(2,1)} %constant.122.pair_ref), custom_call_target="tpu_custom_call" | custom-call | tf_op jit(solution)/shard_map/mix_rows/pallas_call | solution.py:334
  66.5 26.2 %sample.1 = f32[2,8192]{1,0:T(2,128)} custom-call(s32[8192]{0:T(1024)} %get-tuple-element.6.place_ref, s32[1,8192]{1,0:T(1,128)} %bitcast.7, f32[2,8,2048,128]{3,2,1,0:T(8,128)} %mix_rows.1.mixed_ref, bf16[128,128]{1,0:T(8,128)(2,1)} %constant.121.clone.lane_ref), custom_call_target="tpu_custom_call" | custom-call | tf_op jit(solution)/shard_map/sample/pallas_call | solution.py:100
  92.7 0.0 copy-done
  92.7 0.1 compare_select_fusion
  92.8 1.5 %broadcast_multiply_fusion = f32[2,8192]{1,0:T(2,128)} fusion(f32[2,8192]{1,0:T(2,128)} %sample.1, f32[8192]{0:T(1024)S(1)} %compare_select_fusion), kind=kLoop, calls=%fused_computation.30 | loop fusion | flops 16384 | bytes 163840 | tf_op jit(solution)/shard_map/mul | solution.py:419
  94.3 10.5 %reduce.1 = f32[2,512]{1,0:T(2,128)} custom-call(f32[16,2,512]{2,1,0:T(2,128)} %bitcast.6), custom_call_target="tpu_custom_call" | custom-call | tf_op jit(solution)/shard_map/reduce/pallas_call | solution.py:386
  104.8 1.3 %copy.10 = f32[2,512]{1,0:T(2,128)} copy(f32[2,512]{1,0:T(2,128)} %reduce.1) | data formatting | bytes 8192
Async XLA Ops:
  5.1 87.5 %copy-start = (s32[8192]{0:T(1024)S(1)}, s32[8192]{0:T(1024)}, u32[]{:S(2)}) copy-start(s32[8192]{0:T(1024)} %param.11) | copy-start | bytes 98308
